TPU v7x, 32 devices: a whole 2x2x4 slice. The times are simulated.
32 devices in a mesh: dp: 4 (over y, x), rows: 8 (over z, core).
Axes of the slice: x: 2, y: 2, z: 4, core: 2. Of those that a mesh axis runs over, the one named last changes fastest.
Arguments:
- scenes: bfloat16 [4, 256, 256, 384], P('dp', 'rows'), may hold values from -6 to 6
- prompt: bfloat16 [256, 256, 384], P('rows'), may hold values from -6 to 6
- cotangent: bfloat16 [4, 256, 256, 384], P('dp', 'rows'), may hold values from -6 to 6
- first_weight: bfloat16 [2, 8, 48, 48], replicated, may hold values from -0.625 to 0.625
- first_bias: float32 [2, 384], replicated, may hold values from -3 to 3
- second_weight: bfloat16 [2, 8, 48, 48], replicated, may hold values from -0.625 to 0.625
- second_bias: float32 [2, 384], replicated, may hold values from -3 to 3
Outputs:
- mixed: bfloat16 [4, 256, 256, 384], P('dp', 'rows')
- prompt_grad: float32 [256, 256, 384], P('rows', 'dp')
All inputs are finite; a program needn't handle non-finite values.
Results may differ from a plain program's by a relative error of at most 0.014.
Values may be sent and summed in bfloat16 or wider, within the bound.
A program may use at most 128 MiB of HBM per device.

v0:
```python
import math

import jax
import jax.numpy as jnp
from jax import lax
from jax.sharding import PartitionSpec as P

H = 256
W = 256
NB = 8
BS = 48
KW = 128


def product(form, left, right):
    return jnp.einsum(form, left, right, preferred_element_type=jnp.float32)


def row_tables():
    grid_index = jnp.arange(W, dtype=jnp.int32)
    mode_index = jnp.arange(KW, dtype=jnp.int32)
    phases = mode_index[:, None] * grid_index[None, :] % W
    angles = phases.astype(jnp.float32) * (2.0 * math.pi / W)
    factor = 1.0 / math.sqrt(W)
    cosine = jnp.cos(angles) * factor
    sines = jnp.sin(angles) * factor
    forward = jnp.stack([cosine, -sines], axis=0).astype(jnp.bfloat16)
    doubled = jnp.where(mode_index == 0, 1.0, 2.0).astype(jnp.float32)[:, None]
    inverse = jnp.stack([doubled * cosine, -doubled * sines], axis=0).astype(jnp.bfloat16)
    return (forward, jnp.transpose(inverse, (2, 0, 1)))


def column_tables():
    grid_index = jnp.arange(H, dtype=jnp.int32)
    phases = grid_index[:, None] * grid_index[None, :] % H
    angles = phases.astype(jnp.float32) * (2.0 * math.pi / H)
    factor = 1.0 / math.sqrt(H)
    cosine = jnp.cos(angles) * factor
    sines = jnp.sin(angles) * factor
    upper = jnp.stack([cosine, sines], axis=1)
    lower = jnp.stack([-sines, cosine], axis=1)
    forward = jnp.stack([upper, lower], axis=0).astype(jnp.bfloat16)
    return (forward, jnp.transpose(forward, (2, 3, 0, 1)))


def complex_block(weights):
    real_part = weights[0]
    imag_part = weights[1]
    first_row = jnp.stack([real_part, imag_part], axis=2)
    second_row = jnp.stack([-imag_part, real_part], axis=2)
    return jnp.stack([first_row, second_row], axis=0)


def spectral_mix(spectrum, first_block, second_block, first_bias, second_bias):
    layout = spectrum.shape
    pieces = spectrum.reshape(layout[:4] + (NB, BS))
    first_pre = product("smqkbi,qbipj->smpkbj", pieces, first_block) + first_bias.reshape(
        2, 1, NB, BS
    )
    hidden = jax.nn.gelu(first_pre, approximate=False).astype(jnp.bfloat16)
    second = product("smqkbi,qbipj->smpkbj", hidden, second_block) + second_bias.reshape(
        2, 1, NB, BS
    )
    return (second.astype(jnp.bfloat16).reshape(layout), first_pre)


def spectral_back(back_out, first_pre, first_block, second_block):
    layout = back_out.shape
    pieces = back_out.reshape(layout[:4] + (NB, BS))
    back_hidden = product("smpkbj,qbipj->smqkbi", pieces, second_block)
    cumulative = 0.5 * (1.0 + lax.erf(first_pre * 0.7071067811865476))
    density = jnp.exp(-0.5 * first_pre * first_pre) * 0.3989422804014327
    back_pre = (back_hidden * (cumulative + first_pre * density)).astype(jnp.bfloat16)
    back_spectrum = product("smpkbj,qbipj->smqkbi", back_pre, first_block)
    return back_spectrum.astype(jnp.bfloat16).reshape(layout)


def on_device(scenes, prompt, cotangent, first_weight, first_bias, second_weight, second_bias):
    row_fwd, row_inv = row_tables()
    column_fwd, column_inv = column_tables()
    first_block = complex_block(first_weight)
    second_block = complex_block(second_weight)
    summed = (scenes.astype(jnp.float32) + prompt.astype(jnp.float32)[None]).astype(jnp.bfloat16)
    row_spec = product("pkn,shnc->shpkc", row_fwd, summed).astype(jnp.bfloat16)
    back_spec = product("npk,shnc->shpkc", row_inv, cotangent).astype(jnp.bfloat16)
    row_cols = lax.all_to_all(row_spec, "rows", split_axis=3, concat_axis=1, tiled=True)
    spectrum = product("pmqh,shqkc->smpkc", column_fwd, row_cols).astype(jnp.bfloat16)
    output_spec, first_pre = spectral_mix(
        spectrum, first_block, second_block, first_bias, second_bias
    )
    grid_cols = product("phqm,smqkc->shpkc", column_inv, output_spec).astype(jnp.bfloat16)
    grid_spec = lax.all_to_all(grid_cols, "rows", split_axis=1, concat_axis=3, tiled=True)
    back_cols = lax.all_to_all(back_spec, "rows", split_axis=3, concat_axis=1, tiled=True)
    back_out = product("qhpm,shqkc->smpkc", column_inv, back_cols).astype(jnp.bfloat16)
    back_spectrum = spectral_back(back_out, first_pre, first_block, second_block)
    grad_cols = product("pmqh,smpkc->shqkc", column_fwd, back_spectrum).astype(jnp.bfloat16)
    back_rows = lax.all_to_all(grad_cols, "rows", split_axis=1, concat_axis=3, tiled=True)
    mixed = (summed.astype(jnp.float32) + product("npk,shpkc->shnc", row_inv, grid_spec)).astype(
        jnp.bfloat16
    )
    grad_terms = cotangent.astype(jnp.float32) + product("pkn,shpkc->shnc", row_fwd, back_rows)
    local_grad = jnp.sum(grad_terms, axis=0)
    prompt_grad = lax.psum_scatter(
        local_grad.astype(jnp.bfloat16), "dp", scatter_dimension=1, tiled=True
    ).astype(jnp.float32)
    return (mixed, prompt_grad)


def solution(mesh):
    return jax.shard_map(
        on_device,
        mesh=mesh,
        in_specs=(
            P("dp", "rows", None, None),
            P("rows", None, None),
            P("dp", "rows", None, None),
            P(),
            P(),
            P(),
            P(),
        ),
        out_specs=(P("dp", "rows", None, None), P("rows", "dp", None)),
        check_vma=False,
    )
```

profile of v0, /device:TPU:0, one launch (start us, length us, event | category | flops | bytes accessed | tf_op | source)
XLA Modules:
  0.0 772.7 jit_solution(1702958454357875702)
XLA Ops:
  7.2 0.5 negate_convert_fusion.1
  7.7 8.7 %copy.116 = bf16[1,32,256,384]{2,3,1,0:T(8,128)(2,1)} copy(bf16[1,32,256,384]{3,2,1,0:T(8,128)(2,1)} %param.7) | data formatting | bytes 12582912 | tf_op args[0]
  16.4 8.6 %copy.117 = bf16[32,256,384]{1,2,0:T(8,128)(2,1)} copy(bf16[32,256,384]{2,1,0:T(8,128)(2,1)} %param.8) | data formatting | bytes 12582912 | tf_op args[1]
  25.0 10.0 %convert_bitcast_fusion.1 = bf16[1,32,2,128,384]{3,4,2,1,0:T(8,128)(2,1)} fusion(bf16[1,32,256,384]{2,3,1,0:T(8,128)(2,1)} %copy.116, bf16[32,256,384]{1,2,0:T(8,128)(2,1)} %copy.117, bf16[1,128,256]{2,1,0:T(8,128)(2,1)S(1)} %get-tuple-element.22, bf16[1,128,256]{2,1,0:T(8,128)(2,1)S(1)} %get-tuple-element.23), kind=kOutput, calls=%fused_computation.65 | convolution fusion | flops 1626603520 | bytes 19005440 | tf_op jit(solution)/shard_map/pkn,shnc->shpkc/dot_general | solution.py:16
  35.1 16.3 %copy.124 = bf16[1,32,2,128,384]{4,2,1,0,3:T(2,128)(2,1)} copy(bf16[1,32,2,128,384]{3,4,2,1,0:T(8,128)(2,1)} %convert_bitcast_fusion.1) | data formatting | bytes 12582912 | tf_op jit(solution)/shard_map/convert_element_type | solution.py:84
  51.4 6.3 all-to-all-start
  57.7 0.5 multiply_convert_fusion.1
  58.3 0.6 copy-done.1
  58.9 4.6 convert_bitcast_fusion
  63.6 6.4 copy.141
  70.0 126.8 %all-to-all-done = bf16[1,32,2,128,384]{4,2,1,0,3:T(2,128)(2,1)} async-done(((bf16[1,32,2,128,384]{4,2,1,0,3:T(2,128)(2,1)}), bf16[1,32,2,128,384]{4,2,1,0,3:T(2,128)(2,1)}, u32[]{:S(2)}, u32[]{:S(2)}) %all-to-all-start) | async-done | bytes 6291488 | tf_op jit(solution)/shard_map/all_to_all | solution.py:86
  196.8 5.3 all-to-all-start.2
  202.2 0.1 copy.215
  202.4 0.1 copy.213
  202.7 1.0 fusion.81
  203.7 1.1 negate_convert_fusion
  205.0 0.9 pad_maximum_fusion
  205.9 8.6 %copy.125 = bf16[1,32,2,128,384]{4,3,2,1,0:T(8,128)(2,1)S(1)} copy(bf16[1,32,2,128,384]{4,2,1,0,3:T(2,128)(2,1)} %all-to-all-done) | data formatting | bytes 12582912 | tf_op jit(solution)/shard_map/all_to_all | solution.py:86
  214.6 0.8 copy.126
  215.4 10.5 %bitcast_convert_fusion.4 = bf16[16,384,2,256]{3,1,2,0:T(8,128)(2,1)} fusion(bf16[256,2,16,384,1]{3,2,1,0,4:T(8,128)(2,1)S(1)} %bitcast.254, bf16[1,256,2,256]{3,1,2,0:T(8,128)(2,1)S(1)} %get-tuple-element.17, bf16[1,256,2,256]{3,1,2,0:T(8,128)(2,1)S(1)} %get-tuple-element.16), kind=kOutput, calls=%fused_computation.24 | convolution fusion | flops 3225419776 | bytes 13107200 | tf_op jit(solution)/shard_map/pmqh,shqkc->smpkc/dot_general | solution.py:16
  225.9 115.1 %all-to-all-done.2 = bf16[1,32,2,128,384]{4,1,2,0,3:T(8,128)(2,1)} async-done(((bf16[1,32,2,128,384]{4,1,2,0,3:T(8,128)(2,1)}), bf16[1,32,2,128,384]{4,1,2,0,3:T(8,128)(2,1)}, u32[]{:S(2)}, u32[]{:S(2)}) %all-to-all-start.2) | async-done | bytes 6291488 | tf_op jit(solution)/shard_map/all_to_all | solution.py:93
  341.0 6.5 copy.142
  347.5 0.8 copy.143
  348.3 10.6 %bitcast_convert_fusion.2 = bf16[16,384,2,256]{3,1,2,0:T(8,128)(2,1)} fusion(bf16[256,2,16,384,1]{3,2,1,0,4:T(8,128)(2,1)S(1)} %bitcast.252, bf16[1,256,2,256]{3,1,2,0:T(8,128)(2,1)S(1)} %get-tuple-element.17, bf16[1,256,2,256]{3,1,2,0:T(8,128)(2,1)S(1)} %get-tuple-element.16), kind=kOutput, calls=%fused_computation.22 | convolution fusion | flops 3225419776 | bytes 13107200 | tf_op jit(solution)/shard_map/qhpm,shqkc->smpkc/dot_general | solution.py:16
  358.9 1.9 fusion.40
  360.8 4.5 copy-done
  365.3 8.2 %fusion.45 = bf16[256,2,16,8,48,1]{0,4,2,1,3,5:T(8,128)(2,1)S(1)} fusion(f32[2,8,48]{2,0,1:T(2,128)S(1)} %copy.129, f32[8,2,48,256,16,1]{3,2,5,4,1,0:T(8,128)S(1)} %fusion.40, bf16[256,2,16,8,48,1]{0,4,3,1,2,5:T(8,128)(2,1)} %bitcast.259, bf16[1,8,48,2,48]{2,4,0,3,1:T(8,128)(2,1)S(1)} %get-tuple-element.19, bf16[1,8,48,2,48]{2,4,0,3,1:T(8,128)(2,1)S(1)} %get-tuple-element.18), kind=kOutput, calls=%fused_computation.67 | convolution fusion | flops 638656512 | bytes 25316352 | tf_op jit(solution)/shard_map/smpkbj,qbipj->smqkbi/dot_general | solution.py:16
  373.5 1.8 fusion.21
  375.4 0.8 copy.150
  376.2 5.4 fusion.22
  381.6 16.4 %copy.153 = bf16[1,256,2,16,384]{4,2,3,0,1:T(2,128)(2,1)} copy(bf16[1,256,2,16,384]{1,4,2,3,0:T(8,128)(2,1)} %fusion.22) | data formatting | bytes 12582912 | tf_op jit(solution)/shard_map/convert_element_type | solution.py:96
  398.0 4.9 all-to-all-start.3
  402.9 8.9 %copy.140 = bf16[1,32,256,384]{2,3,1,0:T(8,128)(2,1)} copy(bf16[1,32,256,384]{3,2,1,0:T(8,128)(2,1)} %param.9) | data formatting | bytes 12582912 | tf_op args[2]
  411.9 31.4 %fusion.11 = bf16[1,256,2,16,8,48]{1,5,3,2,4,0:T(8,128)(2,1)S(1)} fusion(f32[2,8,48]{2,0,1:T(2,128)S(1)} %copy.131, bf16[1,8,48,2,48]{2,4,0,3,1:T(8,128)(2,1)S(1)} %get-tuple-element.19, bf16[1,8,48,2,48]{2,4,0,3,1:T(8,128)(2,1)S(1)} %get-tuple-element.18, f32[2,8,48]{2,0,1:T(2,128)S(1)} %copy.129, f32[8,2,48,256,16,1]{3,2,5,4,1,0:T(8,128)} %copy-done), kind=kOutput, calls=%fused_computation.16 | convolution fusion | flops 818184192 | bytes 19027968 | tf_op jit(solution)/shard_map/smqkbi,qbipj->smpkbj/dot_general | solution.py:16
  443.4 3.5 copy.132
  446.9 94.9 %all-to-all-done.3 = bf16[1,256,2,16,384]{4,2,3,0,1:T(2,128)(2,1)} async-done(((bf16[1,256,2,16,384]{4,2,3,0,1:T(2,128)(2,1)}), bf16[1,256,2,16,384]{4,2,3,0,1:T(2,128)(2,1)}, u32[]{:S(2)}, u32[]{:S(2)}) %all-to-all-start.3) | async-done | bytes 6291488 | tf_op jit(solution)/shard_map/all_to_all | solution.py:97
  541.8 3.9 copy.154
  545.8 3.9 copy.155
  549.6 7.3 fusion.23
  556.9 9.1 %copy.157 = bf16[32,256,384]{2,0,1:T(8,128)(2,1)} copy(bf16[32,256,384]{1,2,0:T(8,128)(2,1)} %fusion.23) | data formatting | bytes 12582912 | tf_op jit(solution)/shard_map/convert_element_type | solution.py:104
  566.1 8.2 %fusion.20 = bf16[1,256,2,16,384]{1,4,2,3,0:T(8,128)(2,1)} fusion(bf16[256,2,16,384,1]{0,3,2,1,4:T(8,128)(2,1)} %bitcast.251, bf16[2,256,2,256,1]{1,3,0,2,4:T(8,128)(2,1)S(1)} %copy-done.9), kind=kOutput, calls=%fused_computation.40 | convolution fusion | flops 3224371200 | bytes 13107200 | tf_op jit(solution)/shard_map/phqm,smqkc->shpkc/dot_general | solution.py:16
  574.3 16.5 %copy.135 = bf16[1,256,2,16,384]{4,2,3,0,1:T(2,128)(2,1)} copy(bf16[1,256,2,16,384]{1,4,2,3,0:T(8,128)(2,1)} %fusion.20) | data formatting | bytes 12582912 | tf_op jit(solution)/shard_map/convert_element_type | solution.py:91
  590.7 143.1 %all_to_all.60 = bf16[1,256,2,16,384]{4,2,3,0,1:T(2,128)(2,1)S(1)} all-to-all(bf16[1,256,2,16,384]{4,2,3,0,1:T(2,128)(2,1)} %copy.135), channel_id=1, replica_groups=mesh['dp'=4,'rows'=8] {'rows'}, dimensions={1} | all-to-all | bytes 12582912 | tf_op jit(solution)/shard_map/all_to_all | solution.py:92
  733.9 4.4 copy.136
  738.3 6.9 copy.137
  745.3 7.8 %fusion.10 = bf16[1,32,256,384]{2,3,1,0:T(8,128)(2,1)} fusion(bf16[32,2,128,384]{3,2,1,0:T(8,128)(2,1)} %bitcast.246, bf16[32,256,384]{1,2,0:T(8,128)(2,1)S(1)} %bitcast.239, bf16[1,32,256,384]{2,3,1,0:T(8,128)(2,1)S(1)} %bitcast.237, bf16[1,128,256]{2,1,0:T(8,128)(2,1)S(1)} %copy-done.2, bf16[1,128,256]{2,1,0:T(8,128)(2,1)S(1)} %copy-done.4), kind=kOutput, calls=%fused_computation.14 | convolution fusion | flops 1632698368 | bytes 25296896 | tf_op jit(solution)/shard_map/npk,shpkc->shnc/dot_general | solution.py:16
  753.2 8.6 %copy.158 = bf16[1,32,256,384]{3,2,1,0:T(8,128)(2,1)} copy(bf16[1,32,256,384]{2,3,1,0:T(8,128)(2,1)} %fusion.10) | data formatting | bytes 12582912
  761.8 3.6 copy.159
  (64 shorter events, 0.9 us)
Async XLA Ops:
  7.7 17.3 %copy-start.5 = (bf16[1,128,256]{2,1,0:T(8,128)(2,1)}, bf16[1,128,256]{2,1,0:T(8,128)(2,1)S(1)}, u32[]{:S(2)}) copy-start(bf16[1,128,256]{2,1,0:T(8,128)(2,1)S(1)} %get-tuple-element.22) | copy-start | bytes 196612
  7.7 17.3 %copy-start.7 = (bf16[1,128,256]{2,1,0:T(8,128)(2,1)}, bf16[1,128,256]{2,1,0:T(8,128)(2,1)S(1)}, u32[]{:S(2)}) copy-start(bf16[1,128,256]{2,1,0:T(8,128)(2,1)S(1)} %get-tuple-element.23) | copy-start | bytes 196612
  51.4 145.4 %all-to-all-start = ((bf16[1,32,2,128,384]{4,2,1,0,3:T(2,128)(2,1)}), bf16[1,32,2,128,384]{4,2,1,0,3:T(2,128)(2,1)}, u32[]{:S(2)}, u32[]{:S(2)}) async-start(bf16[1,32,2,128,384]{4,2,1,0,3:T(2,128)(2,1)} %copy.124), calls=%async_computation | async-start | bytes 12582912 | tf_op jit(solution)/shard_map/all_to_all | solution.py:86
  58.3 0.6 copy-start.1
  58.3 0.6 copy-start.3
  63.5 138.5 %copy-start.10 = (bf16[2,8,48,48]{3,2,1,0:T(8,128)(2,1)S(1)}, bf16[2,8,48,48]{3,2,1,0:T(8,128)(2,1)}, u32[]{:S(2)}) copy-start(bf16[2,8,48,48]{3,2,1,0:T(8,128)(2,1)} %param.10) | copy-start | bytes 221188
  63.5 138.8 %copy-start.11 = (bf16[2,8,48,48]{3,2,1,0:T(8,128)(2,1)S(1)}, bf16[2,8,48,48]{3,2,1,0:T(8,128)(2,1)}, u32[]{:S(2)}) copy-start(bf16[2,8,48,48]{3,2,1,0:T(8,128)(2,1)} %param.12) | copy-start | bytes 221188
  63.5 139.0 %copy-start.12 = (f32[2,384]{1,0:T(2,128)S(1)}, f32[2,384]{1,0:T(2,128)}, u32[]{:S(2)}) copy-start(f32[2,384]{1,0:T(2,128)} %param.11) | copy-start | bytes 9220
  196.8 144.2 %all-to-all-start.2 = ((bf16[1,32,2,128,384]{4,1,2,0,3:T(8,128)(2,1)}), bf16[1,32,2,128,384]{4,1,2,0,3:T(8,128)(2,1)}, u32[]{:S(2)}, u32[]{:S(2)}) async-start(bf16[1,32,2,128,384]{4,1,2,0,3:T(8,128)(2,1)} %copy.141), calls=%async_computation.2 | async-start | bytes 12582912 | tf_op jit(solution)/shard_map/all_to_all | solution.py:93
  347.5 11.4 %slice-start.6 = ((s8[6291456]{0:T(1024)(128)(4,1)}), s8[2097152]{0:T(1024)(128)(4,1)S(1)}, s32[]{:S(2)}) async-start(s8[6291456]{0:T(1024)(128)(4,1)} %bitcast.248), calls=%async_computation.12 | async-start | bytes 4194304
  348.3 10.6 %slice-start.7 = ((s8[6291456]{0:T(1024)(128)(4,1)}), s8[4194304]{0:T(1024)(128)(4,1)S(1)}, s32[]{:S(2)}) async-start(s8[6291456]{0:T(1024)(128)(4,1)} %bitcast.248), calls=%async_computation.13 | async-start | bytes 8388608
  360.8 4.5 copy-start
  398.0 13.9 %copy-start.13 = (f32[2,384]{1,0:T(2,128)S(1)}, f32[2,384]{1,0:T(2,128)}, u32[]{:S(2)}) copy-start(f32[2,384]{1,0:T(2,128)} %param.13) | copy-start | bytes 9220
  398.0 143.8 %all-to-all-start.3 = ((bf16[1,256,2,16,384]{4,2,3,0,1:T(2,128)(2,1)}), bf16[1,256,2,16,384]{4,2,3,0,1:T(2,128)(2,1)}, u32[]{:S(2)}, u32[]{:S(2)}) async-start(bf16[1,256,2,16,384]{4,2,3,0,1:T(2,128)(2,1)} %copy.153), calls=%async_computation.3 | async-start | bytes 12582912 | tf_op jit(solution)/shard_map/all_to_all | solution.py:97
  402.9 358.9 %reduce-scatter.2.cloned.1.call-start = ((), (), s32[]{:S(2)}) async-start(), calls=%async_computation.5 | async-start | bytes 7864320 | tf_op jit(solution)/shard_map/reduce_scatter | solution.py:103
  446.9 102.7 %slice-start.4 = ((s8[6291456]{0:T(1024)(128)(4,1)}), s8[2097152]{0:T(1024)(128)(4,1)S(1)}, s32[]{:S(2)}) async-start(s8[6291456]{0:T(1024)(128)(4,1)} %bitcast.244), calls=%async_computation.10 | async-start | bytes 4194304
  446.9 102.7 %copy-start.6 = (bf16[1,128,256]{2,1,0:T(8,128)(2,1)S(1)}, bf16[1,128,256]{2,1,0:T(8,128)(2,1)}, u32[]{:S(2)}) copy-start(bf16[1,128,256]{2,1,0:T(8,128)(2,1)} %copy-done.5) | copy-start | bytes 196612
  446.9 102.7 %copy-start.8 = (bf16[1,128,256]{2,1,0:T(8,128)(2,1)S(1)}, bf16[1,128,256]{2,1,0:T(8,128)(2,1)}, u32[]{:S(2)}) copy-start(bf16[1,128,256]{2,1,0:T(8,128)(2,1)} %copy-done.7) | copy-start | bytes 196612
  545.8 3.9 slice-start.5
  556.9 9.1 %copy-start.9 = (bf16[2,256,2,256,1]{1,3,0,2,4:T(8,128)(2,1)S(1)}, bf16[2,256,2,256,1]{1,3,0,2,4:T(8,128)(2,1)}, u32[]{:S(2)}) copy-start(bf16[2,256,2,256,1]{1,3,0,2,4:T(8,128)(2,1)} %get-tuple-element.11) | copy-start | bytes 1572868
  733.9 11.4 %slice-start = ((s8[6291456]{0:T(1024)(128)(4,1)}), s8[4194304]{0:T(1024)(128)(4,1)S(1)}, s32[]{:S(2)}) async-start(s8[6291456]{0:T(1024)(128)(4,1)} %bitcast.236), calls=%async_computation.6 | async-start | bytes 8388608
  733.9 11.4 %slice-start.2 = ((s8[6291456]{0:T(1024)(128)(4,1)}), s8[4194304]{0:T(1024)(128)(4,1)S(1)}, s32[]{:S(2)}) async-start(s8[6291456]{0:T(1024)(128)(4,1)} %bitcast.238), calls=%async_computation.8 | async-start | bytes 8388608
  733.9 11.4 %copy-start.2 = (bf16[1,128,256]{2,1,0:T(8,128)(2,1)S(1)}, bf16[1,128,256]{2,1,0:T(8,128)(2,1)}, u32[]{:S(2)}) copy-start(bf16[1,128,256]{2,1,0:T(8,128)(2,1)} %copy-done.1) | copy-start | bytes 196612
  733.9 11.4 %copy-start.4 = (bf16[1,128,256]{2,1,0:T(8,128)(2,1)S(1)}, bf16[1,128,256]{2,1,0:T(8,128)(2,1)}, u32[]{:S(2)}) copy-start(bf16[1,128,256]{2,1,0:T(8,128)(2,1)} %copy-done.3) | copy-start | bytes 196612
  738.3 7.0 slice-start.1
  738.3 7.0 slice-start.3
Sparse Core Ops, SparseCore 0:
  566.2 69.1 reduce-scatter.1
where the time goes:
time: 782 us; the launch traced here: 773 us
  waiting for transfers between devices  337 us (43%)
  local copies, waits for them, and re-layouts  149 us (19%)
  blocking collectives  143 us (18%)
  matrix products  108 us (14%)
  starting transfers between devices  16.5 us (2%)
  between operations  14.9 us (2%)
    all_to_all x1, blocking collectives, on_device(): lax.all_to_all(grid_cols, 'rows', split_axis=1, concat_axis=3, tiled=True)  143 us
    all_to_all x1, waiting for transfers between devices, on_device(): lax.all_to_all(row_spec, 'rows', split_axis=3, concat_axis=1, tiled=True)  127 us
    all_to_all x1, waiting for transfers between devices, on_device(): lax.all_to_all(back_spec, 'rows', split_axis=3, concat_axis=1, tiled=True)  115 us
    dot_general x12, matrix products, product(): return jnp.einsum(form, left, right, preferred_element_type=jnp.float32)  108 us
    all_to_all x1, waiting for transfers between devices, on_device(): lax.all_to_all(grad_cols, 'rows', split_axis=1, concat_axis=3, tiled=True)  94.9 us
    unnamed x53, local copies, waits for them, and re-layouts  44.1 us
    convert_element_type x1, local copies, waits for them, and re-layouts, on_device(): product('phqm,smqkc->shpkc', column_inv, output_spec).astype(jnp.bfloat16)  16.5 us
    convert_element_type x1, local copies, waits for them, and re-layouts, on_device(): product('pmqh,smpkc->shqkc', column_fwd, back_spectrum).astype(jnp.bfloat16)  16.4 us
  transfers between devices with their start and end apart: 4, of which 3 were waited for; matrix products, arithmetic and copies ran while one was open for 17% of the time, Pallas kernels for 0%

commit v1 on v0

v1 whole, which is shorter than its diff:
```python
import functools
import math

import jax
import jax.numpy as jnp
from jax import lax
from jax.experimental import pallas as pl
from jax.experimental.pallas import tpu as pltpu
from jax.sharding import PartitionSpec as P

VMEM_LIMIT = 48 * 1024 * 1024
HBLOCK = 16


def dot(left, right):
    return jnp.dot(left, right, preferred_element_type=jnp.float32)


def row_tables(width, kept):
    grid_index = jnp.arange(width, dtype=jnp.int32)
    mode_index = jnp.arange(kept, dtype=jnp.int32)
    phases = mode_index[:, None] * grid_index[None, :] % width
    angles = phases.astype(jnp.float32) * (2.0 * math.pi / width)
    factor = 1.0 / math.sqrt(width)
    cosine = jnp.cos(angles) * factor
    sines = jnp.sin(angles) * factor
    forward = jnp.stack([cosine, -sines], axis=0).astype(jnp.bfloat16)
    doubled = jnp.where(mode_index == 0, 1.0, 2.0).astype(jnp.float32)[:, None]
    inverse = jnp.stack([doubled * cosine, -doubled * sines], axis=0).astype(jnp.bfloat16)
    return forward, inverse


def column_tables(height):
    grid_index = jnp.arange(height, dtype=jnp.int32)
    phases = grid_index[:, None] * grid_index[None, :] % height
    angles = phases.astype(jnp.float32) * (2.0 * math.pi / height)
    factor = 1.0 / math.sqrt(height)
    cosine = (jnp.cos(angles) * factor).astype(jnp.bfloat16)
    sines = (jnp.sin(angles) * factor).astype(jnp.bfloat16)
    forward = jnp.block([[cosine, sines], [-sines, cosine]])
    return forward, forward.T


def by_owner(table, owners):
    two, kept, width = table.shape
    split = table.reshape(two, owners, kept // owners, width)
    return split.transpose(1, 0, 2, 3).reshape(two * kept, width)


def block_matrix(weights):
    _, blocks, size, _ = weights.shape
    real, imag = weights[0], weights[1]
    eye = jnp.eye(blocks, dtype=weights.dtype)

    def spread(w):
        full = eye[:, None, :, None] * w[:, :, None, :]
        return full.reshape(blocks * size, blocks * size)

    return jnp.block([[spread(real), spread(imag)], [spread(-imag), spread(real)]])


def params(steps):
    return pltpu.CompilerParams(vmem_limit_bytes=VMEM_LIMIT, dimension_semantics=("arbitrary",) * steps)


def cost(flops, nbytes, trans=0):
    return pl.CostEstimate(flops=int(flops), bytes_accessed=int(nbytes), transcendentals=int(trans))


def full_spec(shape):
    return pl.BlockSpec(shape, lambda i: (0,) * len(shape))


def row_forward(table, arrays, owners):
    h, n, c = arrays[0].shape
    pk = table.shape[0]
    hb = min(HBLOCK, h)
    count = len(arrays)

    def kernel(table_ref, *refs):
        ins, out_ref, held = refs[:count], refs[count], refs[count + 1]
        for j in range(hb):
            if count == 2:
                x = (ins[0][j].astype(jnp.float32) + ins[1][j].astype(jnp.float32)).astype(jnp.bfloat16)
            else:
                x = ins[0][j]
            held[j] = dot(table_ref[...], x)
        part = pk // owners
        for o in range(owners):
            piece = held[:, o * part : (o + 1) * part, :]
            out_ref[o] = jnp.swapaxes(piece, 0, 1).astype(jnp.bfloat16)

    return pl.pallas_call(
        kernel,
        grid=(h // hb,),
        in_specs=[full_spec(table.shape)] + [pl.BlockSpec((hb, n, c), lambda i: (i, 0, 0))] * count,
        out_specs=pl.BlockSpec((owners, pk // owners, hb, c), lambda i: (0, 0, i, 0)),
        out_shape=jax.ShapeDtypeStruct((owners, pk // owners, h, c), jnp.bfloat16),
        scratch_shapes=[pltpu.VMEM((hb, pk, c), jnp.float32)],
        compiler_params=params(1),
        cost_estimate=cost(2 * h * pk * n * c, 2 * h * n * c * (count + 1)),
        name="row_forward%d" % count,
    )(table, *arrays)


def row_inverse(table, spec, arrays, pieces):
    owners, part, h, c = spec.shape
    n, pk = table.shape
    hb = min(HBLOCK, h)
    count = len(arrays)
    wide = n // pieces

    def kernel(table_ref, spec_ref, *refs):
        ins, out_ref, held = refs[:count], refs[count], refs[count + 1]
        for o in range(owners):
            piece = spec_ref[o].astype(jnp.float32)
            held[:, o * part : (o + 1) * part, :] = jnp.swapaxes(piece, 0, 1)
        for j in range(hb):
            y = dot(table_ref[...], held[j].astype(jnp.bfloat16))
            if count == 2:
                x = ins[0][j].astype(jnp.float32) + ins[1][j].astype(jnp.float32)
                y = y + x.astype(jnp.bfloat16).astype(jnp.float32)
            elif count == 1:
                y = y + ins[0][j].astype(jnp.float32)
            for d in range(pieces):
                out_ref[d, j] = y[d * wide : (d + 1) * wide].astype(jnp.bfloat16)

    return pl.pallas_call(
        kernel,
        grid=(h // hb,),
        in_specs=[
            full_spec(table.shape),
            pl.BlockSpec((owners, part, hb, c), lambda i: (0, 0, i, 0)),
        ]
        + [pl.BlockSpec((hb, n, c), lambda i: (i, 0, 0))] * count,
        out_specs=pl.BlockSpec((pieces, hb, wide, c), lambda i: (0, i, 0, 0)),
        out_shape=jax.ShapeDtypeStruct((pieces, h, wide, c), jnp.bfloat16),
        scratch_shapes=[pltpu.VMEM((hb, pk, c), jnp.float32)],
        compiler_params=params(1),
        cost_estimate=cost(2 * h * pk * n * c, 2 * h * n * c * (count + 2)),
        name="row_inverse%d" % count,
    )(table, spec, *arrays)


def stacked(ref):
    owners, _, _, h, c = ref.shape
    return jnp.concatenate([ref[:, q, 0].reshape(owners * h, c) for q in range(2)], axis=0)


def beside(x):
    half = x.shape[0] // 2
    return jnp.concatenate([x[:half], x[half:]], axis=1)


def above(x):
    half = x.shape[1] // 2
    return jnp.concatenate([x[:, :half], x[:, half:]], axis=0)


def column_forward(spec, forward, inverse, first, second, first_bias, second_bias):
    owners, two, kept, h, c = spec.shape
    rows = owners * h

    def kernel(x_ref, f_ref, i_ref, m1_ref, m2_ref, b1_ref, b2_ref, out_ref, slope_ref):
        spectrum = dot(f_ref[...], stacked(x_ref)).astype(jnp.bfloat16)
        z = dot(beside(spectrum), m1_ref[...]) + b1_ref[...]
        cumulative = 0.5 * (1.0 + lax.erf(z * 0.7071067811865476))
        hidden = (z * cumulative).astype(jnp.bfloat16)
        slope_ref[0] = cumulative + z * (jnp.exp(-0.5 * z * z) * 0.3989422804014327)
        mixed = (dot(hidden, m2_ref[...]) + b2_ref[...]).astype(jnp.bfloat16)
        grid = dot(i_ref[...], above(mixed)).astype(jnp.bfloat16)
        for q in range(2):
            out_ref[:, q, 0] = grid[q * rows : (q + 1) * rows].reshape(owners, h, c)

    block = pl.BlockSpec((owners, two, 1, h, c), lambda i: (0, 0, i, 0, 0))
    return pl.pallas_call(
        kernel,
        grid=(kept,),
        in_specs=[block]
        + [full_spec(a.shape) for a in (forward, inverse, first, second, first_bias, second_bias)],
        out_specs=[block, pl.BlockSpec((1, rows, 2 * c), lambda i: (i, 0, 0))],
        out_shape=[
            jax.ShapeDtypeStruct(spec.shape, jnp.bfloat16),
            jax.ShapeDtypeStruct((kept, rows, 2 * c), jnp.float32),
        ],
        compiler_params=params(1),
        cost_estimate=cost(kept * (16 * rows * rows * c + 16 * rows * c * c), 16 * kept * rows * c, 4 * kept * rows * c),
        name="column_forward",
    )(spec, forward, inverse, first, second, first_bias, second_bias)


def column_backward(spec, slope, forward, first_t, second_t, inverse=None):
    owners, two, kept, h, c = spec.shape
    rows = owners * h
    extra = () if inverse is None else (inverse,)

    def kernel(x_ref, s_ref, f_ref, m1_ref, m2_ref, *refs):
        out_ref = refs[-1]
        back_out = dot(f_ref[...], stacked(x_ref)).astype(jnp.bfloat16)
        back_pre = (dot(beside(back_out), m2_ref[...]) * s_ref[0]).astype(jnp.bfloat16)
        back = above(dot(back_pre, m1_ref[...]).astype(jnp.bfloat16))
        if inverse is None:
            out_ref[0] = back
        else:
            grid = dot(refs[0][...], back).astype(jnp.bfloat16)
            for q in range(2):
                out_ref[:, q, 0] = grid[q * rows : (q + 1) * rows].reshape(owners, h, c)

    block = pl.BlockSpec((owners, two, 1, h, c), lambda i: (0, 0, i, 0, 0))
    flat = pl.BlockSpec((1, 2 * rows, c), lambda i: (i, 0, 0))
    return pl.pallas_call(
        kernel,
        grid=(kept,),
        in_specs=[block, pl.BlockSpec((1, rows, 2 * c), lambda i: (i, 0, 0))]
        + [full_spec(a.shape) for a in (forward, first_t, second_t) + extra],
        out_specs=flat if inverse is None else block,
        out_shape=jax.ShapeDtypeStruct((kept, 2 * rows, c) if inverse is None else spec.shape, jnp.bfloat16),
        compiler_params=params(1),
        cost_estimate=cost(kept * (8 * rows * rows * c + 16 * rows * c * c), 16 * kept * rows * c),
        name="column_backward",
    )(spec, slope, forward, first_t, second_t, *extra)


def column_summed(spec, inverse, owners, groups):
    kept, double, c = spec.shape
    rows = double // 2
    h = rows // owners // groups

    def kernel(x_ref, i_ref, out_ref):
        grid = dot(i_ref[...], x_ref[0])
        for q in range(2):
            part = grid[q * rows : (q + 1) * rows].reshape(owners, groups, h, c)
            for d in range(groups):
                out_ref[d, :, q, 0] = part[:, d].astype(jnp.bfloat16)

    return pl.pallas_call(
        kernel,
        grid=(kept,),
        in_specs=[pl.BlockSpec((1, double, c), lambda i: (i, 0, 0)), full_spec(inverse.shape)],
        out_specs=pl.BlockSpec((groups, owners, 2, 1, h, c), lambda i: (0, 0, 0, i, 0, 0)),
        out_shape=jax.ShapeDtypeStruct((groups, owners, 2, kept, h, c), jnp.bfloat16),
        compiler_params=params(1),
        cost_estimate=cost(kept * 8 * rows * rows * c, 8 * kept * rows * c),
        name="column_summed",
    )(spec, inverse)


def exchange(x, axis):
    return lax.all_to_all(x, axis, split_axis=0, concat_axis=0, tiled=True)


def on_device(groups, owners, scenes, prompt, cotangent, first_weight, first_bias, second_weight, second_bias):
    _, h, n, c = scenes.shape
    height = h * owners
    kept = n // 2
    own = kept // owners
    forward, inverse = row_tables(n, kept)
    fwd_rows, inv_rows = by_owner(forward, owners), by_owner(inverse, owners)
    column_fwd, column_inv = column_tables(height)
    first, second = block_matrix(first_weight), block_matrix(second_weight)
    scene, cot = scenes[0], cotangent[0]
    shape5 = (owners, 2, own, h, c)

    row_spec = row_forward(fwd_rows, [scene, prompt], owners)
    row_spec, cot_in = lax.optimization_barrier((row_spec, cot))
    row_cols = exchange(row_spec, "rows").reshape(shape5)
    back_spec = row_forward(inv_rows, [cot_in], owners)
    back_cols = exchange(back_spec, "rows").reshape(shape5)
    grid_cols, slope = column_forward(
        row_cols, column_fwd, column_inv, first, second, first_bias.reshape(1, -1), second_bias.reshape(1, -1)
    )
    grid_spec = exchange(grid_cols, "rows").reshape(owners, 2 * own, h, c)
    summable = own % groups == 0 and h % (8 * groups) == 0
    if summable:
        back = column_backward(back_cols, slope, column_fwd, first.T, second.T)
        total = lax.psum_scatter(back, "dp", scatter_dimension=0, tiled=True)
        cot_total = lax.psum_scatter(cot, "dp", scatter_dimension=1, tiled=True)
        grad_cols = column_summed(total, column_inv, owners, groups)
        few, low = own // groups, h // groups
        back_rows = exchange(grad_cols.reshape(groups * owners, 2 * few, low, c), ("dp", "rows"))
        table = forward.reshape(2, owners, groups, few, n).transpose(4, 2, 1, 0, 3).reshape(n, 2 * kept)
        grad = row_inverse(table, back_rows, [], groups)
        grad = exchange(grad, "dp").reshape(h, n // groups, c)
        prompt_grad = cot_total.astype(jnp.float32) + grad.astype(jnp.float32)
    else:
        grad_cols = column_backward(back_cols, slope, column_fwd, first.T, second.T, column_inv)
        back_rows = exchange(grad_cols, "rows").reshape(owners, 2 * own, h, c)
        local = row_inverse(fwd_rows.T, back_rows, [cot], 1)[0]
        prompt_grad = lax.psum_scatter(local, "dp", scatter_dimension=1, tiled=True).astype(jnp.float32)
    mixed = row_inverse(inv_rows.T, grid_spec, [scene, prompt], 1)
    return mixed, prompt_grad


def solution(mesh):
    return jax.shard_map(
        functools.partial(on_device, mesh.shape["dp"], mesh.shape["rows"]),
        mesh=mesh,
        in_specs=(
            P("dp", "rows", None, None),
            P("rows", None, None),
            P("dp", "rows", None, None),
            P(),
            P(),
            P(),
            P(),
        ),
        out_specs=(P("dp", "rows", None, None), P("rows", "dp", None)),
        check_vma=False,
    )
```

time: 782 us -> 626 us (0.80)
  blocking collectives: 143 us -> 0 us
  waiting for transfers between devices: 337 us -> 466 us
  local copies, waits for them, and re-layouts: 149 us -> 22.7 us
  matrix products: 108 us -> 0 us
  Pallas kernels: 0 us -> 84.5 us
  other arithmetic: 4.29 us -> 12.9 us
  starting transfers between devices: 16.5 us -> 24.6 us
    all_to_all x1 -> x0, blocking collectives: 143 us -> none  [on_device(): lax.all_to_all(grid_cols, 'rows', split_axis=1, concat_axis=3, tiled=True)]
    dot_general x12 -> x0, matrix products: 108 us -> none  [product(): return jnp.einsum(form, left, right, preferred_element_type=jnp.float32)]
    pallas_call x0 -> x7, Pallas kernels: none -> 84.5 us  [the longest x1 27.6 us: column_forward(): pl.pallas_call(kernel, grid=(kept,), in_specs=[block] + [full_spec(a.shap...]
    reduce_scatter x1 -> x2, waiting for transfers between devices: 0.01 us -> 69.3 us  [the longest x1 69.2 us: on_device(): total = lax.psum_scatter(back, 'dp', scatter_dimension=0, tiled=True)]
    convert_element_type x7 -> x0, local copies, waits for them, and re-layouts: 69 us -> none  [the longest x1 16.5 us: on_device(): product('phqm,smqkc->shpkc', column_inv, output_spec).astype(jnp.bfloat16)]
    all_to_all x3 -> x5, waiting for transfers between devices: 337 us -> 396 us  [exchange(): return lax.all_to_all(x, axis, split_axis=0, concat_axis=0, tiled=True)]
    unnamed x53 -> x20, local copies, waits for them, and re-layouts: 44.1 us -> 5.24 us
    all_to_all x8 -> x0, local copies, waits for them, and re-layouts: 35.9 us -> none  [the longest x2 11.4 us: on_device(): lax.all_to_all(grid_cols, 'rows', split_axis=1, concat_axis=3, tiled=True)]
  transfers between devices with their start and end apart: 4 -> 7, of which waited for: 3 -> 6; matrix products, arithmetic and copies ran while one was open for 17% -> 4% of each run, Pallas kernels for 0% -> 8%
where the time goes in v1:
time: 626 us; the launch traced here: 625 us
  waiting for transfers between devices  466 us (74%)
  Pallas kernels  84.5 us (13%)
  starting transfers between devices  24.6 us (4%)
  local copies, waits for them, and re-layouts  22.7 us (4%)
  between operations  14.3 us (2%)
  other arithmetic  12.9 us (2%)
    all_to_all x5, waiting for transfers between devices, exchange(): return lax.all_to_all(x, axis, split_axis=0, concat_axis=0, tiled=True)  396 us
    reduce_scatter x1, waiting for transfers between devices, on_device(): total = lax.psum_scatter(back, 'dp', scatter_dimension=0, tiled=True)  69.2 us
    pallas_call x1, Pallas kernels, column_forward(): pl.pallas_call(kernel, grid=(kept,), in_specs=[block] + [full_spec(a.shap...  27.6 us
    all_to_all x5, starting transfers between devices, exchange(): return lax.all_to_all(x, axis, split_axis=0, concat_axis=0, tiled=True)  24.3 us
    pallas_call x1, Pallas kernels, column_backward(): pl.pallas_call(kernel, grid=(kept,), in_specs=[block, pl.BlockSpec((1, ro...  22.8 us
    pallas_call x2, Pallas kernels, row_forward(): pl.pallas_call(kernel, grid=(h // hb,), in_specs=[full_spec(table.shape)]...  17.3 us
    pallas_call x2, Pallas kernels, row_inverse(): pl.pallas_call(kernel, grid=(h // hb,), in_specs=[full_spec(table.shape),...  14 us
  transfers between devices with their start and end apart: 7, of which 6 were waited for; matrix products, arithmetic and copies ran while one was open for 4% of the time, Pallas kernels for 8%

profile of v1, /device:TPU:0, one launch (start us, length us, event | category | flops | bytes accessed | tf_op | source)
XLA Modules:
  0.0 624.5 jit_solution(1052527221571414207)
XLA Ops:
  7.2 0.6 multiply_convert_fusion.3
  7.9 9.3 %row_forward2.1 = bf16[8,32,32,384]{3,2,1,0:T(8,128)(2,1)} custom-call(bf16[256,256]{1,0:T(8,128)(2,1)S(1)} %bitcast.71, bf16[32,256,384]{2,1,0:T(8,128)(2,1)} %bitcast.76, bf16[32,256,384]{2,1,0:T(8,128)(2,1)} %refs_1_.3), custom_call_target="tpu_custom_call" | custom-call | flops 1610612736 | bytes 18874368 | tf_op jit(solution)/shard_map/row_forward2/pallas_call | solution.py:93
  17.2 6.3 %all-to-all-start = ((bf16[8,32,32,384]{3,2,1,0:T(8,128)(2,1)}), bf16[8,32,32,384]{3,2,1,0:T(8,128)(2,1)}, u32[]{:S(2)}, u32[]{:S(2)}) async-start(bf16[8,32,32,384]{3,2,1,0:T(8,128)(2,1)} %row_forward2.1), calls=%async_computation | async-start | bytes 12582912 | tf_op jit(solution)/shard_map/all_to_all | solution.py:249
  23.5 8.0 %row_forward1.1 = bf16[8,32,32,384]{3,2,1,0:T(8,128)(2,1)} custom-call(bf16[256,256]{1,0:T(8,128)(2,1)S(1)} %bitcast.69, bf16[32,256,384]{2,1,0:T(8,128)(2,1)} %bitcast.74), custom_call_target="tpu_custom_call" | custom-call | flops 1610612736 | bytes 12582912 | tf_op jit(solution)/shard_map/row_forward1/pallas_call | solution.py:93
  31.5 131.0 %all-to-all-done = bf16[8,32,32,384]{3,2,1,0:T(8,128)(2,1)} async-done(((bf16[8,32,32,384]{3,2,1,0:T(8,128)(2,1)}), bf16[8,32,32,384]{3,2,1,0:T(8,128)(2,1)}, u32[]{:S(2)}, u32[]{:S(2)}) %all-to-all-start) | async-done | bytes 6291488 | tf_op jit(solution)/shard_map/all_to_all | solution.py:249
  162.5 4.8 all-to-all-start.2
  167.4 0.2 reduce-scatter.5.cloned.1.call-start
  167.6 0.1 copy.32
  167.8 0.1 copy.33
  167.9 0.7 copy.35
  168.7 0.8 copy.36
  169.4 0.8 copy.34
  170.2 0.8 copy.37
  171.0 2.7 broadcast_multiply_fusion.1
  173.6 2.4 mul.470
  176.1 2.4 mul.474
  178.5 1.3 mul.477
  179.8 1.3 mul.481
  181.0 1.2 mul.485
  182.3 1.3 mul.488
  183.5 3.1 fusion.26
  186.7 2.4 copy.39.m1_ref
  189.0 1.4 copy.40.m2_ref
  190.5 1.0 fusion.20
  191.5 1.1 multiply_convert_fusion
  192.7 0.2 copy.38.f_ref
  192.9 1.3 copy-done.2
  194.2 1.3 copy-done.3
  195.5 27.6 %column_forward.1 = (bf16[8,2,16,32,384]{4,3,2,1,0:T(8,128)(2,1)}, f32[16,256,768]{2,1,0:T(8,128)}) custom-call(bf16[8,2,16,32,384]{4,3,2,1,0:T(8,128)(2,1)} %bitcast.7.x_ref, bf16[512,512]{1,0:T(8,128)(2,1)S(1)} %copy.38.f_ref, bf16[512,512]{1,0:T(8,128)(2,1)S(1)} %get-tuple-element.14.i_ref, bf16[768,768]{1,0:T(8,128)(2,1)S(1)} %copy-done.2, ...), custom_call_target="tpu_custom_call" | custom-call | flops 16106127360 | bytes 25165824 | tf_op jit(solution)/shard_map/column_forward/pallas_call | solution.py:176
  223.1 83.2 %all-to-all-done.2 = bf16[8,32,32,384]{3,2,1,0:T(8,128)(2,1)} async-done(((bf16[8,32,32,384]{3,2,1,0:T(8,128)(2,1)}), bf16[8,32,32,384]{3,2,1,0:T(8,128)(2,1)}, u32[]{:S(2)}, u32[]{:S(2)}) %all-to-all-start.2) | async-done | bytes 6291488 | tf_op jit(solution)/shard_map/all_to_all | solution.py:249
  306.3 1.3 copy-done.1
  307.6 22.8 %column_backward.1 = bf16[16,512,384]{2,1,0:T(8,128)(2,1)} custom-call(bf16[8,2,16,32,384]{4,3,2,1,0:T(8,128)(2,1)} %bitcast.16.x_ref, f32[16,256,768]{2,1,0:T(8,128)} %get-tuple-element.9.s_ref, bf16[512,512]{1,0:T(8,128)(2,1)S(1)} %copy.38.f_ref, bf16[768,768]{1,0:T(8,128)(2,1)S(1)} %copy-done.1, bf16[768,768]{1,0:T(8,128)(2,1)S(1)} %get-tuple-element.10.m2_ref), custom_call_target="tpu_custom_call" | custom-call | flops 12884901888 | bytes 25165824 | tf_op jit(solution)/shard_map/column_backward/pallas_call | solution.py:211
  330.4 69.2 %reduce-scatter.5.cloned.1.call-done.x_ref = bf16[4,512,384]{2,1,0:T(8,128)(2,1)} async-done(((bf16[16,512,384]{2,1,0:T(8,128)(2,1)}), bf16[4,512,384]{2,1,0:T(8,128)(2,1)}) %reduce-scatter.5.cloned.1.call-update) | async-done | bytes 1572880 | tf_op jit(solution)/shard_map/reduce_scatter | solution.py:276
  399.6 1.4 copy-done
  401.0 2.8 column_summed.1
  403.9 4.6 all-to-all-start.3
  408.5 0.7 reduce-scatter.3.cloned.1.call-update
  409.2 38.2 %all-to-all-done.3.spec_ref = bf16[32,8,8,384]{3,2,1,0:T(8,128)(2,1)S(1)} async-done(((bf16[32,8,8,384]{3,2,1,0:T(8,128)(2,1)}), bf16[32,8,8,384]{3,2,1,0:T(8,128)(2,1)S(1)}, u32[]{:S(2)}, u32[]{:S(2)}) %all-to-all-start.3) | async-done | bytes 1572896 | tf_op jit(solution)/shard_map/all_to_all | solution.py:249
  447.5 5.0 all-to-all-start.1
  452.5 0.6 multiply_convert_fusion.2
  453.2 0.1 copy.44.table_ref
  453.3 2.3 row_inverse0.1
  455.7 135.5 %all-to-all-done.1 = bf16[8,2,16,32,384]{4,3,2,1,0:T(8,128)(2,1)} async-done(((bf16[8,2,16,32,384]{4,3,2,1,0:T(8,128)(2,1)}), bf16[8,2,16,32,384]{4,3,2,1,0:T(8,128)(2,1)}, u32[]{:S(2)}, u32[]{:S(2)}) %all-to-all-start.1) | async-done | bytes 6291488 | tf_op jit(solution)/shard_map/all_to_all | solution.py:249
  591.2 3.6 all-to-all-start.4
  594.8 0.1 copy.41.table_ref
  594.9 11.6 %row_inverse2.1 = bf16[1,32,256,384]{3,2,1,0:T(8,128)(2,1)} custom-call(bf16[256,256]{1,0:T(8,128)(2,1)S(1)} %copy.41.table_ref, bf16[8,32,32,384]{3,2,1,0:T(8,128)(2,1)} %bitcast.13.spec_ref, bf16[32,256,384]{2,1,0:T(8,128)(2,1)} %bitcast.77, bf16[32,256,384]{2,1,0:T(8,128)(2,1)} %refs_1_.3), custom_call_target="tpu_custom_call" | custom-call | flops 1610612736 | bytes 25165824 | tf_op jit(solution)/shard_map/row_inverse2/pallas_call | solution.py:128
  606.5 7.5 %all-to-all-done.4 = bf16[4,8,64,384]{3,2,1,0:T(8,128)(2,1)S(1)} async-done(((bf16[4,8,64,384]{3,2,1,0:T(8,128)(2,1)}), bf16[4,8,64,384]{3,2,1,0:T(8,128)(2,1)S(1)}, u32[]{:S(2)}, u32[]{:S(2)}) %all-to-all-start.4) | async-done | bytes 1572896 | tf_op jit(solution)/shard_map/all_to_all | solution.py:249
  614.1 3.6 convert_add_fusion
  (33 shorter events, 0.4 us)
Async XLA Ops:
  17.2 145.4 %all-to-all-start = ((bf16[8,32,32,384]{3,2,1,0:T(8,128)(2,1)}), bf16[8,32,32,384]{3,2,1,0:T(8,128)(2,1)}, u32[]{:S(2)}, u32[]{:S(2)}) async-start(bf16[8,32,32,384]{3,2,1,0:T(8,128)(2,1)} %row_forward2.1), calls=%async_computation | async-start | bytes 12582912 | tf_op jit(solution)/shard_map/all_to_all | solution.py:249
  31.5 136.1 %copy-start.5 = (bf16[2,8,48,48]{3,2,1,0:T(8,128)(2,1)S(1)}, bf16[2,8,48,48]{3,2,1,0:T(8,128)(2,1)}, u32[]{:S(2)}) copy-start(bf16[2,8,48,48]{3,2,1,0:T(8,128)(2,1)} %param.10) | copy-start | bytes 221188
  31.5 136.4 %copy-start.6 = (bf16[2,8,48,48]{3,2,1,0:T(8,128)(2,1)S(1)}, bf16[2,8,48,48]{3,2,1,0:T(8,128)(2,1)}, u32[]{:S(2)}) copy-start(bf16[2,8,48,48]{3,2,1,0:T(8,128)(2,1)} %param.12) | copy-start | bytes 221188
  162.5 143.8 %all-to-all-start.2 = ((bf16[8,32,32,384]{3,2,1,0:T(8,128)(2,1)}), bf16[8,32,32,384]{3,2,1,0:T(8,128)(2,1)}, u32[]{:S(2)}, u32[]{:S(2)}) async-start(bf16[8,32,32,384]{3,2,1,0:T(8,128)(2,1)} %row_forward1.1), calls=%async_computation.3 | async-start | bytes 12582912 | tf_op jit(solution)/shard_map/all_to_all | solution.py:249
  167.4 232.3 %reduce-scatter.5.cloned.1.call-start = ((), (), s32[]{:S(2)}) async-start(), calls=%async_computation.8 | async-start | bytes 7864320 | tf_op jit(solution)/shard_map/reduce_scatter | solution.py:276
  179.8 3.8 copy-start.4
  189.0 3.9 copy-start.7
  189.0 3.9 copy-start.8
  192.9 1.3 copy-start.2
  194.2 1.3 copy-start.3
  306.3 1.3 copy-start.1
  399.6 1.4 copy-start
  403.9 43.6 %all-to-all-start.3 = ((bf16[32,8,8,384]{3,2,1,0:T(8,128)(2,1)}), bf16[32,8,8,384]{3,2,1,0:T(8,128)(2,1)S(1)}, u32[]{:S(2)}, u32[]{:S(2)}) async-start(bf16[32,8,8,384]{3,2,1,0:T(8,128)(2,1)} %bitcast.19), calls=%async_computation.5 | async-start | bytes 3145728 | tf_op jit(solution)/shard_map/all_to_all | solution.py:249
  408.5 198.0 %reduce-scatter.3.cloned.1.call-start = ((), (), s32[]{:S(2)}) async-start(), calls=%async_computation.7 | async-start | bytes 7864320 | tf_op jit(solution)/shard_map/reduce_scatter | solution.py:277
  447.5 143.7 %all-to-all-start.1 = ((bf16[8,2,16,32,384]{4,3,2,1,0:T(8,128)(2,1)}), bf16[8,2,16,32,384]{4,3,2,1,0:T(8,128)(2,1)}, u32[]{:S(2)}, u32[]{:S(2)}) async-start(bf16[8,2,16,32,384]{4,3,2,1,0:T(8,128)(2,1)} %get-tuple-element.7), calls=%async_computation.1 | async-start | bytes 12582912 | tf_op jit(solution)/shard_map/all_to_all | solution.py:249
  591.2 22.9 %all-to-all-start.4 = ((bf16[4,8,64,384]{3,2,1,0:T(8,128)(2,1)}), bf16[4,8,64,384]{3,2,1,0:T(8,128)(2,1)S(1)}, u32[]{:S(2)}, u32[]{:S(2)}) async-start(bf16[4,8,64,384]{3,2,1,0:T(8,128)(2,1)} %row_inverse0.1), calls=%async_computation.6 | async-start | bytes 3145728 | tf_op jit(solution)/shard_map/all_to_all | solution.py:249
Sparse Core Ops, SparseCore 0:
  330.5 69.0 reduce-scatter.4
  412.3 78.9 reduce-scatter.2

commit v2 on v1

--- a/solution.py
+++ b/solution.py
@@ -272,10 +272,12 @@
     grid_spec = exchange(grid_cols, "rows").reshape(owners, 2 * own, h, c)
     summable = own % groups == 0 and h % (8 * groups) == 0
     if summable:
+        cot_total = lax.psum_scatter(cot, "dp", scatter_dimension=1, tiled=True)
+        back_cols, cot_total = lax.optimization_barrier((back_cols, cot_total))
         back = column_backward(back_cols, slope, column_fwd, first.T, second.T)
         total = lax.psum_scatter(back, "dp", scatter_dimension=0, tiled=True)
-        cot_total = lax.psum_scatter(cot, "dp", scatter_dimension=1, tiled=True)
         grad_cols = column_summed(total, column_inv, owners, groups)
+        grad_cols, grid_spec = lax.optimization_barrier((grad_cols, grid_spec))
         few, low = own // groups, h // groups
         back_rows = exchange(grad_cols.reshape(groups * owners, 2 * few, low, c), ("dp", "rows"))
         table = forward.reshape(2, owners, groups, few, n).transpose(4, 2, 1, 0, 3).reshape(n, 2 * kept)

time: 626 us -> 552 us (0.88)
  waiting for transfers between devices: 466 us -> 394 us
    all_to_all x5, waiting for transfers between devices: 396 us -> 329 us  [exchange(): return lax.all_to_all(x, axis, split_axis=0, concat_axis=0, tiled=True)]
  transfers between devices with their start and end apart: 7 -> 7, of which waited for: 6 -> 6; matrix products, arithmetic and copies ran while one was open for 4% -> 5% of each run, Pallas kernels for 8% -> 9%
where the time goes in v2:
time: 552 us; the launch traced here: 551 us
  waiting for transfers between devices  394 us (71%)
  Pallas kernels  84.7 us (15%)
  starting transfers between devices  23.5 us (4%)
  local copies, waits for them, and re-layouts  22.7 us (4%)
  between operations  14.3 us (3%)
  other arithmetic  11.6 us (2%)
    all_to_all x5, waiting for transfers between devices, exchange(): return lax.all_to_all(x, axis, split_axis=0, concat_axis=0, tiled=True)  329 us
    reduce_scatter x1, waiting for transfers between devices, on_device(): total = lax.psum_scatter(back, 'dp', scatter_dimension=0, tiled=True)  64.5 us
    pallas_call x1, Pallas kernels, column_forward(): pl.pallas_call(kernel, grid=(kept,), in_specs=[block] + [full_spec(a.shap...  27.6 us
    all_to_all x5, starting transfers between devices, exchange(): return lax.all_to_all(x, axis, split_axis=0, concat_axis=0, tiled=True)  23.2 us
    pallas_call x1, Pallas kernels, column_backward(): pl.pallas_call(kernel, grid=(kept,), in_specs=[block, pl.BlockSpec((1, ro...  22.8 us
    pallas_call x2, Pallas kernels, row_forward(): pl.pallas_call(kernel, grid=(h // hb,), in_specs=[full_spec(table.shape)]...  17.4 us
    pallas_call x2, Pallas kernels, row_inverse(): pl.pallas_call(kernel, grid=(h // hb,), in_specs=[full_spec(table.shape),...  14.1 us
    mul x12, local copies, waits for them, and re-layouts, spread(): full = eye[:, None, :, None] * w[:, :, None, :]  11.7 us
  transfers between devices with their start and end apart: 7, of which 6 were waited for; matrix products, arithmetic and copies ran while one was open for 5% of the time, Pallas kernels for 9%

profile of v2, /device:TPU:0, one launch (start us, length us, event | category | flops | bytes accessed | tf_op | source)
XLA Modules:
  0.0 550.9 jit_solution(11899564566044729672)
XLA Ops:
  7.2 0.6 multiply_convert_fusion.3
  7.9 9.3 %row_forward2.1 = bf16[8,32,32,384]{3,2,1,0:T(8,128)(2,1)} custom-call(bf16[256,256]{1,0:T(8,128)(2,1)S(1)} %bitcast.71, bf16[32,256,384]{2,1,0:T(8,128)(2,1)} %bitcast.76, bf16[32,256,384]{2,1,0:T(8,128)(2,1)} %refs_1_.3), custom_call_target="tpu_custom_call" | custom-call | flops 1610612736 | bytes 18874368 | tf_op jit(solution)/shard_map/row_forward2/pallas_call | solution.py:93
  17.2 6.3 %all-to-all-start.1 = ((bf16[8,32,32,384]{3,2,1,0:T(8,128)(2,1)}), bf16[8,32,32,384]{3,2,1,0:T(8,128)(2,1)}, u32[]{:S(2)}, u32[]{:S(2)}) async-start(bf16[8,32,32,384]{3,2,1,0:T(8,128)(2,1)} %row_forward2.1), calls=%async_computation.2 | async-start | bytes 12582912 | tf_op jit(solution)/shard_map/all_to_all | solution.py:249
  23.5 0.7 reduce-scatter.3.cloned.1.call-update
  24.2 8.1 %row_forward1.1 = bf16[8,32,32,384]{3,2,1,0:T(8,128)(2,1)} custom-call(bf16[256,256]{1,0:T(8,128)(2,1)S(1)} %bitcast.68, bf16[32,256,384]{2,1,0:T(8,128)(2,1)} %bitcast.75), custom_call_target="tpu_custom_call" | custom-call | flops 1610612736 | bytes 12582912 | tf_op jit(solution)/shard_map/row_forward1/pallas_call | solution.py:93
  32.3 130.2 %all-to-all-done.1 = bf16[8,32,32,384]{3,2,1,0:T(8,128)(2,1)} async-done(((bf16[8,32,32,384]{3,2,1,0:T(8,128)(2,1)}), bf16[8,32,32,384]{3,2,1,0:T(8,128)(2,1)}, u32[]{:S(2)}, u32[]{:S(2)}) %all-to-all-start.1) | async-done | bytes 6291488 | tf_op jit(solution)/shard_map/all_to_all | solution.py:249
  162.5 4.8 all-to-all-start
  167.4 0.2 reduce-scatter.5.cloned.1.call-start
  167.6 0.1 copy.34
  167.8 0.1 copy.35
  167.9 0.8 copy.37
  168.7 0.8 copy.38
  169.5 0.8 copy.36
  170.3 0.8 copy.39
  171.0 2.7 broadcast_multiply_fusion.1
  173.7 2.4 mul.470
  176.1 2.4 mul.474
  178.5 1.2 mul.477
  179.8 1.3 mul.481
  181.0 1.2 mul.485
  182.3 1.2 mul.488
  183.5 3.1 fusion.26
  186.6 2.4 copy.41.m1_ref
  189.0 1.4 copy.42.m2_ref
  190.5 1.0 fusion.20
  191.5 1.1 multiply_convert_fusion
  192.7 0.2 copy.40.f_ref
  192.9 1.3 copy-done.2
  194.2 1.3 copy-done.3
  195.5 27.6 %column_forward.1 = (bf16[8,2,16,32,384]{4,3,2,1,0:T(8,128)(2,1)}, f32[16,256,768]{2,1,0:T(8,128)}) custom-call(bf16[8,2,16,32,384]{4,3,2,1,0:T(8,128)(2,1)} %bitcast.9.x_ref, bf16[512,512]{1,0:T(8,128)(2,1)S(1)} %copy.40.f_ref, bf16[512,512]{1,0:T(8,128)(2,1)S(1)} %get-tuple-element.22.i_ref, bf16[768,768]{1,0:T(8,128)(2,1)S(1)} %copy-done.2, ...), custom_call_target="tpu_custom_call" | custom-call | flops 16106127360 | bytes 25165824 | tf_op jit(solution)/shard_map/column_forward/pallas_call | solution.py:176
  223.1 83.3 %all-to-all-done = bf16[8,32,32,384]{3,2,1,0:T(8,128)(2,1)} async-done(((bf16[8,32,32,384]{3,2,1,0:T(8,128)(2,1)}), bf16[8,32,32,384]{3,2,1,0:T(8,128)(2,1)}, u32[]{:S(2)}, u32[]{:S(2)}) %all-to-all-start) | async-done | bytes 6291488 | tf_op jit(solution)/shard_map/all_to_all | solution.py:249
  306.3 1.3 copy-done.1
  307.6 22.8 %column_backward.1 = bf16[16,512,384]{2,1,0:T(8,128)(2,1)} custom-call(bf16[8,2,16,32,384]{4,3,2,1,0:T(8,128)(2,1)} %bitcast.8.x_ref, f32[16,256,768]{2,1,0:T(8,128)} %get-tuple-element.13.s_ref, bf16[512,512]{1,0:T(8,128)(2,1)S(1)} %copy.40.f_ref, bf16[768,768]{1,0:T(8,128)(2,1)S(1)} %copy-done.1, bf16[768,768]{1,0:T(8,128)(2,1)S(1)} %get-tuple-element.18.m2_ref), custom_call_target="tpu_custom_call" | custom-call | flops 12884901888 | bytes 25165824 | tf_op jit(solution)/shard_map/column_backward/pallas_call | solution.py:211
  330.4 4.8 all-to-all-start.2
  335.2 64.5 %reduce-scatter.5.cloned.1.call-done.x_ref = bf16[4,512,384]{2,1,0:T(8,128)(2,1)} async-done(((bf16[16,512,384]{2,1,0:T(8,128)(2,1)}), bf16[4,512,384]{2,1,0:T(8,128)(2,1)}) %reduce-scatter.5.cloned.1.call-update) | async-done | bytes 1572880 | tf_op jit(solution)/shard_map/reduce_scatter | solution.py:278
  399.6 1.4 copy-done
  401.0 2.8 column_summed.1
  403.9 70.3 %all-to-all-done.2 = bf16[8,2,16,32,384]{4,3,2,1,0:T(8,128)(2,1)} async-done(((bf16[8,2,16,32,384]{4,3,2,1,0:T(8,128)(2,1)}), bf16[8,2,16,32,384]{4,3,2,1,0:T(8,128)(2,1)}, u32[]{:S(2)}, u32[]{:S(2)}) %all-to-all-start.2) | async-done | bytes 6291488 | tf_op jit(solution)/shard_map/all_to_all | solution.py:249
  474.1 3.7 all-to-all-start.3
  477.8 0.6 multiply_convert_fusion.2
  478.6 0.1 copy.45.table_ref
  478.7 37.8 %all-to-all-done.3.spec_ref = bf16[32,8,8,384]{3,2,1,0:T(8,128)(2,1)S(1)} async-done(((bf16[32,8,8,384]{3,2,1,0:T(8,128)(2,1)}), bf16[32,8,8,384]{3,2,1,0:T(8,128)(2,1)S(1)}, u32[]{:S(2)}, u32[]{:S(2)}) %all-to-all-start.3) | async-done | bytes 1572896 | tf_op jit(solution)/shard_map/all_to_all | solution.py:249
  516.5 2.3 row_inverse0.1
  518.8 3.6 all-to-all-start.4
  522.4 0.1 copy.33
  522.5 11.8 %row_inverse2.1 = bf16[1,32,256,384]{3,2,1,0:T(8,128)(2,1)} custom-call(bf16[256,256]{1,0:T(8,128)(2,1)S(1)} %bitcast.70, bf16[8,32,32,384]{3,2,1,0:T(8,128)(2,1)} %bitcast.17.spec_ref, bf16[32,256,384]{2,1,0:T(8,128)(2,1)} %bitcast.77, bf16[32,256,384]{2,1,0:T(8,128)(2,1)} %refs_1_.3), custom_call_target="tpu_custom_call" | custom-call | flops 1610612736 | bytes 25165824 | tf_op jit(solution)/shard_map/row_inverse2/pallas_call | solution.py:128
  534.3 7.5 %all-to-all-done.4 = bf16[4,8,64,384]{3,2,1,0:T(8,128)(2,1)S(1)} async-done(((bf16[4,8,64,384]{3,2,1,0:T(8,128)(2,1)}), bf16[4,8,64,384]{3,2,1,0:T(8,128)(2,1)S(1)}, u32[]{:S(2)}, u32[]{:S(2)}) %all-to-all-start.4) | async-done | bytes 1572896 | tf_op jit(solution)/shard_map/all_to_all | solution.py:249
  541.7 2.4 convert_add_fusion
  (35 shorter events, 0.4 us)
Async XLA Ops:
  17.2 145.4 %all-to-all-start.1 = ((bf16[8,32,32,384]{3,2,1,0:T(8,128)(2,1)}), bf16[8,32,32,384]{3,2,1,0:T(8,128)(2,1)}, u32[]{:S(2)}, u32[]{:S(2)}) async-start(bf16[8,32,32,384]{3,2,1,0:T(8,128)(2,1)} %row_forward2.1), calls=%async_computation.2 | async-start | bytes 12582912 | tf_op jit(solution)/shard_map/all_to_all | solution.py:249
  23.5 282.8 %reduce-scatter.3.cloned.1.call-start = ((), (), s32[]{:S(2)}) async-start(), calls=%async_computation.7 | async-start | bytes 7864320 | tf_op jit(solution)/shard_map/reduce_scatter | solution.py:275
  32.3 135.3 %copy-start.6 = (bf16[2,8,48,48]{3,2,1,0:T(8,128)(2,1)S(1)}, bf16[2,8,48,48]{3,2,1,0:T(8,128)(2,1)}, u32[]{:S(2)}) copy-start(bf16[2,8,48,48]{3,2,1,0:T(8,128)(2,1)} %param.10) | copy-start | bytes 221188
  32.3 135.6 %copy-start.7 = (bf16[2,8,48,48]{3,2,1,0:T(8,128)(2,1)S(1)}, bf16[2,8,48,48]{3,2,1,0:T(8,128)(2,1)}, u32[]{:S(2)}) copy-start(bf16[2,8,48,48]{3,2,1,0:T(8,128)(2,1)} %param.12) | copy-start | bytes 221188
  162.5 143.8 %all-to-all-start = ((bf16[8,32,32,384]{3,2,1,0:T(8,128)(2,1)}), bf16[8,32,32,384]{3,2,1,0:T(8,128)(2,1)}, u32[]{:S(2)}, u32[]{:S(2)}) async-start(bf16[8,32,32,384]{3,2,1,0:T(8,128)(2,1)} %row_forward1.1), calls=%async_computation | async-start | bytes 12582912 | tf_op jit(solution)/shard_map/all_to_all | solution.py:249
  167.4 232.3 %reduce-scatter.5.cloned.1.call-start = ((), (), s32[]{:S(2)}) async-start(), calls=%async_computation.8 | async-start | bytes 7864320 | tf_op jit(solution)/shard_map/reduce_scatter | solution.py:278
  179.8 3.7 copy-start.5
  189.0 3.9 copy-start.8
  189.0 3.9 copy-start.9
  192.9 1.3 copy-start.2
  194.2 1.3 copy-start.3
  306.3 1.3 copy-start.1
  330.4 143.7 %all-to-all-start.2 = ((bf16[8,2,16,32,384]{4,3,2,1,0:T(8,128)(2,1)}), bf16[8,2,16,32,384]{4,3,2,1,0:T(8,128)(2,1)}, u32[]{:S(2)}, u32[]{:S(2)}) async-start(bf16[8,2,16,32,384]{4,3,2,1,0:T(8,128)(2,1)} %get-tuple-element.14), calls=%async_computation.4 | async-start | bytes 12582912 | tf_op jit(solution)/shard_map/all_to_all | solution.py:249
  399.6 1.4 copy-start
  474.1 42.4 %all-to-all-start.3 = ((bf16[32,8,8,384]{3,2,1,0:T(8,128)(2,1)}), bf16[32,8,8,384]{3,2,1,0:T(8,128)(2,1)S(1)}, u32[]{:S(2)}, u32[]{:S(2)}) async-start(bf16[32,8,8,384]{3,2,1,0:T(8,128)(2,1)} %bitcast.19), calls=%async_computation.5 | async-start | bytes 3145728 | tf_op jit(solution)/shard_map/all_to_all | solution.py:249
  518.8 22.9 %all-to-all-start.4 = ((bf16[4,8,64,384]{3,2,1,0:T(8,128)(2,1)}), bf16[4,8,64,384]{3,2,1,0:T(8,128)(2,1)S(1)}, u32[]{:S(2)}, u32[]{:S(2)}) async-start(bf16[4,8,64,384]{3,2,1,0:T(8,128)(2,1)} %row_inverse0.1), calls=%async_computation.6 | async-start | bytes 3145728 | tf_op jit(solution)/shard_map/all_to_all | solution.py:249
  522.5 19.2 %copy-start.4 = (bf16[32,64,384]{2,1,0:T(8,128)(2,1)S(1)}, bf16[32,64,384]{2,1,0:T(8,128)(2,1)}, u32[]{:S(2)}) copy-start(bf16[32,64,384]{2,1,0:T(8,128)(2,1)} %reduce-scatter.3.cloned.1.call-done) | copy-start | bytes 4718596
Sparse Core Ops, SparseCore 0:
  27.3 71.6 reduce-scatter.2
  330.5 69.0 reduce-scatter.4

commit v3 on v2

--- a/solution.py
+++ b/solution.py
@@ -71,6 +71,11 @@
     return pl.BlockSpec(shape, lambda i: (0,) * len(shape))
 
 
+def spans(widths):
+    ends = [sum(widths[: i + 1]) for i in range(len(widths))]
+    return list(zip([0] + ends[:-1], ends))
+
+
 def row_forward(table, arrays, owners):
     h, n, c = arrays[0].shape
     pk = table.shape[0]
@@ -103,18 +108,23 @@
     )(table, *arrays)
 
 
-def row_inverse(table, spec, arrays, pieces):
-    owners, part, h, c = spec.shape
+def row_inverse(table, specs, arrays, pieces):
+    owners, part, h, _ = specs[0].shape
+    lanes = spans([spec.shape[-1] for spec in specs])
+    c = lanes[-1][1]
+    cut = len(specs)
     n, pk = table.shape
     hb = min(HBLOCK, h)
     count = len(arrays)
     wide = n // pieces
 
-    def kernel(table_ref, spec_ref, *refs):
+    def kernel(table_ref, *refs):
+        spec_refs, refs = refs[:cut], refs[cut:]
         ins, out_ref, held = refs[:count], refs[count], refs[count + 1]
-        for o in range(owners):
-            piece = spec_ref[o].astype(jnp.float32)
-            held[:, o * part : (o + 1) * part, :] = jnp.swapaxes(piece, 0, 1)
+        for spec_ref, (low, high) in zip(spec_refs, lanes):
+            for o in range(owners):
+                piece = spec_ref[o].astype(jnp.float32)
+                held[:, o * part : (o + 1) * part, low:high] = jnp.swapaxes(piece, 0, 1)
         for j in range(hb):
             y = dot(table_ref[...], held[j].astype(jnp.bfloat16))
             if count == 2:
@@ -128,10 +138,8 @@
     return pl.pallas_call(
         kernel,
         grid=(h // hb,),
-        in_specs=[
-            full_spec(table.shape),
-            pl.BlockSpec((owners, part, hb, c), lambda i: (0, 0, i, 0)),
-        ]
+        in_specs=[full_spec(table.shape)]
+        + [pl.BlockSpec((owners, part, hb, high - low), lambda i: (0, 0, i, 0)) for low, high in lanes]
         + [pl.BlockSpec((hb, n, c), lambda i: (i, 0, 0))] * count,
         out_specs=pl.BlockSpec((pieces, hb, wide, c), lambda i: (0, i, 0, 0)),
         out_shape=jax.ShapeDtypeStruct((pieces, h, wide, c), jnp.bfloat16),
@@ -139,7 +147,7 @@
         compiler_params=params(1),
         cost_estimate=cost(2 * h * pk * n * c, 2 * h * n * c * (count + 2)),
         name="row_inverse%d" % count,
-    )(table, spec, *arrays)
+    )(table, *specs, *arrays)
 
 
 def stacked(ref):
@@ -157,11 +165,13 @@
     return jnp.concatenate([x[:, :half], x[:, half:]], axis=0)
 
 
-def column_forward(spec, forward, inverse, first, second, first_bias, second_bias):
+def column_forward(spec, forward, inverse, first, second, first_bias, second_bias, widths):
     owners, two, kept, h, c = spec.shape
+    lanes = spans(widths)
     rows = owners * h
 
-    def kernel(x_ref, f_ref, i_ref, m1_ref, m2_ref, b1_ref, b2_ref, out_ref, slope_ref):
+    def kernel(x_ref, f_ref, i_ref, m1_ref, m2_ref, b1_ref, b2_ref, *out_refs):
+        slope_ref = out_refs[-1]
         spectrum = dot(f_ref[...], stacked(x_ref)).astype(jnp.bfloat16)
         z = dot(beside(spectrum), m1_ref[...]) + b1_ref[...]
         cumulative = 0.5 * (1.0 + lax.erf(z * 0.7071067811865476))
@@ -169,20 +179,21 @@
         slope_ref[0] = cumulative + z * (jnp.exp(-0.5 * z * z) * 0.3989422804014327)
         mixed = (dot(hidden, m2_ref[...]) + b2_ref[...]).astype(jnp.bfloat16)
         grid = dot(i_ref[...], above(mixed)).astype(jnp.bfloat16)
-        for q in range(2):
-            out_ref[:, q, 0] = grid[q * rows : (q + 1) * rows].reshape(owners, h, c)
+        for out_ref, (low, high) in zip(out_refs, lanes):
+            for q in range(2):
+                piece = grid[q * rows : (q + 1) * rows, low:high]
+                out_ref[:, q, 0] = piece.reshape(owners, h, high - low)
 
     block = pl.BlockSpec((owners, two, 1, h, c), lambda i: (0, 0, i, 0, 0))
+    outs = [pl.BlockSpec((owners, two, 1, h, w), lambda i: (0, 0, i, 0, 0)) for w in widths]
     return pl.pallas_call(
         kernel,
         grid=(kept,),
         in_specs=[block]
         + [full_spec(a.shape) for a in (forward, inverse, first, second, first_bias, second_bias)],
-        out_specs=[block, pl.BlockSpec((1, rows, 2 * c), lambda i: (i, 0, 0))],
-        out_shape=[
-            jax.ShapeDtypeStruct(spec.shape, jnp.bfloat16),
-            jax.ShapeDtypeStruct((kept, rows, 2 * c), jnp.float32),
-        ],
+        out_specs=outs + [pl.BlockSpec((1, rows, 2 * c), lambda i: (i, 0, 0))],
+        out_shape=[jax.ShapeDtypeStruct((owners, two, kept, h, w), jnp.bfloat16) for w in widths]
+        + [jax.ShapeDtypeStruct((kept, rows, 2 * c), jnp.float32)],
         compiler_params=params(1),
         cost_estimate=cost(kept * (16 * rows * rows * c + 16 * rows * c * c), 16 * kept * rows * c, 4 * kept * rows * c),
         name="column_forward",
@@ -266,29 +277,35 @@
     row_cols = exchange(row_spec, "rows").reshape(shape5)
     back_spec = row_forward(inv_rows, [cot_in], owners)
     back_cols = exchange(back_spec, "rows").reshape(shape5)
-    grid_cols, slope = column_forward(
-        row_cols, column_fwd, column_inv, first, second, first_bias.reshape(1, -1), second_bias.reshape(1, -1)
+    lead = 128 if c > 128 else c // 2
+    biases = first_bias.reshape(1, -1), second_bias.reshape(1, -1)
+    lead_cols, rest_cols, slope = column_forward(
+        row_cols, column_fwd, column_inv, first, second, *biases, (lead, c - lead)
     )
-    grid_spec = exchange(grid_cols, "rows").reshape(owners, 2 * own, h, c)
+    grid_lead = exchange(lead_cols, "rows")
     summable = own % groups == 0 and h % (8 * groups) == 0
     if summable:
         cot_total = lax.psum_scatter(cot, "dp", scatter_dimension=1, tiled=True)
         back_cols, cot_total = lax.optimization_barrier((back_cols, cot_total))
         back = column_backward(back_cols, slope, column_fwd, first.T, second.T)
+        rest_cols, grid_lead, back = lax.optimization_barrier((rest_cols, grid_lead, back))
+        grid_rest = exchange(rest_cols, "rows")
         total = lax.psum_scatter(back, "dp", scatter_dimension=0, tiled=True)
         grad_cols = column_summed(total, column_inv, owners, groups)
-        grad_cols, grid_spec = lax.optimization_barrier((grad_cols, grid_spec))
+        grad_cols, grid_rest = lax.optimization_barrier((grad_cols, grid_rest))
         few, low = own // groups, h // groups
         back_rows = exchange(grad_cols.reshape(groups * owners, 2 * few, low, c), ("dp", "rows"))
         table = forward.reshape(2, owners, groups, few, n).transpose(4, 2, 1, 0, 3).reshape(n, 2 * kept)
-        grad = row_inverse(table, back_rows, [], groups)
+        grad = row_inverse(table, [back_rows], [], groups)
         grad = exchange(grad, "dp").reshape(h, n // groups, c)
         prompt_grad = cot_total.astype(jnp.float32) + grad.astype(jnp.float32)
     else:
+        grid_rest = exchange(rest_cols, "rows")
         grad_cols = column_backward(back_cols, slope, column_fwd, first.T, second.T, column_inv)
         back_rows = exchange(grad_cols, "rows").reshape(owners, 2 * own, h, c)
-        local = row_inverse(fwd_rows.T, back_rows, [cot], 1)[0]
+        local = row_inverse(fwd_rows.T, [back_rows], [cot], 1)[0]
         prompt_grad = lax.psum_scatter(local, "dp", scatter_dimension=1, tiled=True).astype(jnp.float32)
+    grid_spec = [part.reshape(owners, 2 * own, h, part.shape[-1]) for part in (grid_lead, grid_rest)]
     mixed = row_inverse(inv_rows.T, grid_spec, [scene, prompt], 1)
     return mixed, prompt_grad
 

time: 552 us -> 540 us (0.978)
  waiting for transfers between devices: 394 us -> 371 us
    all_to_all x5 -> x6, waiting for transfers between devices: 329 us -> 306 us  [exchange(): return lax.all_to_all(x, axis, split_axis=0, concat_axis=0, tiled=True)]
    all_to_all x5 -> x6, starting transfers between devices: 23.2 us -> 27.4 us  [exchange(): return lax.all_to_all(x, axis, split_axis=0, concat_axis=0, tiled=True)]
  transfers between devices with their start and end apart: 7 -> 8, of which waited for: 6 -> 7; matrix products, arithmetic and copies ran while one was open for 5% -> 5% of each run, Pallas kernels for 9% -> 13%
where the time goes in v3:
time: 540 us; the launch traced here: 538 us
  waiting for transfers between devices  371 us (69%)
  Pallas kernels  83.7 us (16%)
  starting transfers between devices  27.7 us (5%)
  local copies, waits for them, and re-layouts  27.5 us (5%)
  between operations  14.3 us (3%)
  other arithmetic  13.8 us (3%)
    all_to_all x6, waiting for transfers between devices, exchange(): return lax.all_to_all(x, axis, split_axis=0, concat_axis=0, tiled=True)  306 us
    reduce_scatter x1, waiting for transfers between devices, on_device(): total = lax.psum_scatter(back, 'dp', scatter_dimension=0, tiled=True)  64.7 us
    pallas_call x1, Pallas kernels, column_forward(): pl.pallas_call(kernel, grid=(kept,), in_specs=[block] + [full_spec(a.shap...  27.6 us
    all_to_all x6, starting transfers between devices, exchange(): return lax.all_to_all(x, axis, split_axis=0, concat_axis=0, tiled=True)  27.4 us
    pallas_call x1, Pallas kernels, column_backward(): pl.pallas_call(kernel, grid=(kept,), in_specs=[block, pl.BlockSpec((1, ro...  22.7 us
    pallas_call x2, Pallas kernels, row_forward(): pl.pallas_call(kernel, grid=(h // hb,), in_specs=[full_spec(table.shape)]...  17.4 us
    pallas_call x2, Pallas kernels, row_inverse(): pl.pallas_call(kernel, grid=(h // hb,), in_specs=[full_spec(table.shape)]...  14.1 us
    mul x12, local copies, waits for them, and re-layouts, spread(): full = eye[:, None, :, None] * w[:, :, None, :]  13.4 us
  transfers between devices with their start and end apart: 8, of which 7 were waited for; matrix products, arithmetic and copies ran while one was open for 5% of the time, Pallas kernels for 13%

profile of v3, /device:TPU:0, one launch (start us, length us, event | category | flops | bytes accessed | tf_op | source)
XLA Modules:
  0.0 538.4 jit_solution(14624305936608309546)
XLA Ops:
  7.2 0.6 multiply_convert_fusion.3
  7.9 9.3 %row_forward2.1 = bf16[8,32,32,384]{3,2,1,0:T(8,128)(2,1)} custom-call(bf16[256,256]{1,0:T(8,128)(2,1)S(1)} %bitcast.74, bf16[32,256,384]{2,1,0:T(8,128)(2,1)} %bitcast.79, bf16[32,256,384]{2,1,0:T(8,128)(2,1)} %refs_3_.1), custom_call_target="tpu_custom_call" | custom-call | flops 1610612736 | bytes 18874368 | tf_op jit(solution)/shard_map/row_forward2/pallas_call | solution.py:98
  17.2 6.3 %all-to-all-start = ((bf16[8,32,32,384]{3,2,1,0:T(8,128)(2,1)}), bf16[8,32,32,384]{3,2,1,0:T(8,128)(2,1)}, u32[]{:S(2)}, u32[]{:S(2)}) async-start(bf16[8,32,32,384]{3,2,1,0:T(8,128)(2,1)} %row_forward2.1), calls=%async_computation | async-start | bytes 12582912 | tf_op jit(solution)/shard_map/all_to_all | solution.py:260
  23.5 8.1 %row_forward1.1 = bf16[8,32,32,384]{3,2,1,0:T(8,128)(2,1)} custom-call(bf16[256,256]{1,0:T(8,128)(2,1)S(1)} %bitcast.71, bf16[32,256,384]{2,1,0:T(8,128)(2,1)} %bitcast.77), custom_call_target="tpu_custom_call" | custom-call | flops 1610612736 | bytes 12582912 | tf_op jit(solution)/shard_map/row_forward1/pallas_call | solution.py:98
  31.6 131.0 %all-to-all-done = bf16[8,32,32,384]{3,2,1,0:T(8,128)(2,1)} async-done(((bf16[8,32,32,384]{3,2,1,0:T(8,128)(2,1)}), bf16[8,32,32,384]{3,2,1,0:T(8,128)(2,1)}, u32[]{:S(2)}, u32[]{:S(2)}) %all-to-all-start) | async-done | bytes 6291488 | tf_op jit(solution)/shard_map/all_to_all | solution.py:260
  162.5 4.8 all-to-all-start.2
  168.1 1.0 fusion.20
  169.1 1.1 multiply_convert_fusion
  170.5 0.8 copy.38
  171.3 0.7 copy.35
  172.1 0.8 copy.36
  172.8 0.7 copy.37
  173.6 0.7 copy.39
  174.4 0.8 copy.34
  175.1 2.7 broadcast_multiply_fusion.1
  177.8 2.5 mul.481
  180.3 2.4 mul.488
  182.7 2.4 mul.485
  185.2 1.3 mul.470
  186.5 1.3 mul.477
  187.7 0.5 mul.474
  188.3 3.5 fusion.26
  191.7 1.6 copy.41.m1_ref
  193.3 1.5 copy.42.m2_ref
  194.8 1.5 copy-done.6
  196.3 27.6 %column_forward.1 = (bf16[8,2,16,32,128]{4,3,2,1,0:T(8,128)(2,1)S(1)}, bf16[8,2,16,32,256]{4,3,2,1,0:T(8,128)(2,1)}, f32[16,256,768]{2,1,0:T(8,128)}) custom-call(bf16[8,2,16,32,384]{4,3,2,1,0:T(8,128)(2,1)} %bitcast.7.x_ref, bf16[512,512]{1,0:T(8,128)(2,1)S(1)} %copy.40.f_ref, bf16[512,512]{1,0:T(8,128)(2,1)S(1)} %get-tuple-element.30.i_ref, ...), custom_call_target="tpu_custom_call" | custom-call | flops 16106127360 | bytes 25165824 | tf_op jit(solution)/shard_map/column_forward/pallas_call | solution.py:189
  223.9 1.3 copy-done.2
  225.2 81.1 %all-to-all-done.2 = bf16[8,32,32,384]{3,2,1,0:T(8,128)(2,1)} async-done(((bf16[8,32,32,384]{3,2,1,0:T(8,128)(2,1)}), bf16[8,32,32,384]{3,2,1,0:T(8,128)(2,1)}, u32[]{:S(2)}, u32[]{:S(2)}) %all-to-all-start.2) | async-done | bytes 6291488 | tf_op jit(solution)/shard_map/all_to_all | solution.py:260
  306.3 3.6 all-to-all-start.1
  310.0 1.3 copy-done.4
  311.2 1.3 copy-done.5
  312.5 22.7 %column_backward.1 = bf16[16,512,384]{2,1,0:T(8,128)(2,1)} custom-call(bf16[8,2,16,32,384]{4,3,2,1,0:T(8,128)(2,1)} %bitcast.14.x_ref, f32[16,256,768]{2,1,0:T(8,128)} %get-tuple-element.19.s_ref, bf16[512,512]{1,0:T(8,128)(2,1)S(1)} %copy.40.f_ref, bf16[768,768]{1,0:T(8,128)(2,1)S(1)} %copy-done.5, bf16[768,768]{1,0:T(8,128)(2,1)S(1)} %copy-done.4), custom_call_target="tpu_custom_call" | custom-call | flops 12884901888 | bytes 25165824 | tf_op jit(solution)/shard_map/column_backward/pallas_call | solution.py:222
  335.2 23.6 %all-to-all-done.1 = bf16[8,2,16,32,128]{4,3,2,1,0:T(8,128)(2,1)S(1)} async-done(((bf16[8,2,16,32,128]{4,3,2,1,0:T(8,128)(2,1)}), bf16[8,2,16,32,128]{4,3,2,1,0:T(8,128)(2,1)S(1)}, u32[]{:S(2)}, u32[]{:S(2)}) %all-to-all-start.1) | async-done | bytes 2097184 | tf_op jit(solution)/shard_map/all_to_all | solution.py:260
  358.9 4.6 all-to-all-start.3
  363.5 64.7 %reduce-scatter.5.cloned.1.call-done.x_ref = bf16[4,512,384]{2,1,0:T(8,128)(2,1)} async-done(((bf16[16,512,384]{2,1,0:T(8,128)(2,1)}), bf16[4,512,384]{2,1,0:T(8,128)(2,1)}) %reduce-scatter.5.cloned.1.call-update) | async-done | bytes 1572880 | tf_op jit(solution)/shard_map/reduce_scatter | solution.py:293
  428.2 1.4 copy-done.3
  429.6 1.9 column_summed.1
  431.5 1.1 copy-done
  432.6 24.8 %all-to-all-done.3 = bf16[8,2,16,32,256]{4,3,2,1,0:T(8,128)(2,1)} async-done(((bf16[8,2,16,32,256]{4,3,2,1,0:T(8,128)(2,1)}), bf16[8,2,16,32,256]{4,3,2,1,0:T(8,128)(2,1)}, u32[]{:S(2)}, u32[]{:S(2)}) %all-to-all-start.3) | async-done | bytes 4194336 | tf_op jit(solution)/shard_map/all_to_all | solution.py:260
  457.5 3.8 all-to-all-start.4
  461.3 0.6 multiply_convert_fusion.2
  462.2 37.8 %all-to-all-done.4.refs_0_ = bf16[32,8,8,384]{3,2,1,0:T(8,128)(2,1)} async-done(((bf16[32,8,8,384]{3,2,1,0:T(8,128)(2,1)}), bf16[32,8,8,384]{3,2,1,0:T(8,128)(2,1)}, u32[]{:S(2)}, u32[]{:S(2)}) %all-to-all-start.4) | async-done | bytes 1572896 | tf_op jit(solution)/shard_map/all_to_all | solution.py:260
  499.9 2.6 row_inverse0.1
  502.6 1.1 copy-done.1
  503.7 4.4 all-to-all-start.5
  508.2 11.5 %row_inverse2.1 = bf16[1,32,256,384]{3,2,1,0:T(8,128)(2,1)} custom-call(bf16[256,256]{1,0:T(8,128)(2,1)S(1)} %bitcast.73, bf16[8,32,32,128]{3,2,1,0:T(8,128)(2,1)S(1)} %bitcast.69, bf16[8,32,32,256]{3,2,1,0:T(8,128)(2,1)} %bitcast.18.refs_1_, bf16[32,256,384]{2,1,0:T(8,128)(2,1)} %bitcast.80, bf16[32,256,384]{2,1,0:T(8,128)(2,1)} %refs_3_.1), custom_call_target="tpu_custom_call" | custom-call | flops 1610612736 | bytes 25165824 | tf_op jit(solution)/shard_map/row_inverse2/pallas_call | solution.py:138
  519.7 7.8 %all-to-all-done.5 = bf16[4,8,64,384]{3,2,1,0:T(8,128)(2,1)} async-done(((bf16[4,8,64,384]{3,2,1,0:T(8,128)(2,1)}), bf16[4,8,64,384]{3,2,1,0:T(8,128)(2,1)}, u32[]{:S(2)}, u32[]{:S(2)}) %all-to-all-start.5) | async-done | bytes 1572896 | tf_op jit(solution)/shard_map/all_to_all | solution.py:260
  527.5 4.1 convert_add_fusion
  (39 shorter events, 1.6 us)
Async XLA Ops:
  17.2 145.4 %all-to-all-start = ((bf16[8,32,32,384]{3,2,1,0:T(8,128)(2,1)}), bf16[8,32,32,384]{3,2,1,0:T(8,128)(2,1)}, u32[]{:S(2)}, u32[]{:S(2)}) async-start(bf16[8,32,32,384]{3,2,1,0:T(8,128)(2,1)} %row_forward2.1), calls=%async_computation | async-start | bytes 12582912 | tf_op jit(solution)/shard_map/all_to_all | solution.py:260
  162.5 143.7 %all-to-all-start.2 = ((bf16[8,32,32,384]{3,2,1,0:T(8,128)(2,1)}), bf16[8,32,32,384]{3,2,1,0:T(8,128)(2,1)}, u32[]{:S(2)}, u32[]{:S(2)}) async-start(bf16[8,32,32,384]{3,2,1,0:T(8,128)(2,1)} %row_forward1.1), calls=%async_computation.2 | async-start | bytes 12582912 | tf_op jit(solution)/shard_map/all_to_all | solution.py:260
  167.3 142.6 %reduce-scatter.3.cloned.1.call-start = ((), (), s32[]{:S(2)}) async-start(), calls=%async_computation.8 | async-start | bytes 7864320 | tf_op jit(solution)/shard_map/reduce_scatter | solution.py:288
  168.1 2.4 copy-start.8
  168.1 3.2 copy-start.7
  191.7 3.1 copy-start.9
  191.7 3.1 copy-start.10
  194.8 1.5 copy-start.6
  223.9 1.3 copy-start.2
  306.3 52.6 %all-to-all-start.1 = ((bf16[8,2,16,32,128]{4,3,2,1,0:T(8,128)(2,1)}), bf16[8,2,16,32,128]{4,3,2,1,0:T(8,128)(2,1)S(1)}, u32[]{:S(2)}, u32[]{:S(2)}) async-start(bf16[8,2,16,32,128]{4,3,2,1,0:T(8,128)(2,1)} %copy-done.2), calls=%async_computation.1 | async-start | bytes 4194304 | tf_op jit(solution)/shard_map/all_to_all | solution.py:260
  309.9 118.3 %reduce-scatter.5.cloned.1.call-start = ((), (), s32[]{:S(2)}) async-start(), calls=%async_computation.9 | async-start | bytes 7864320 | tf_op jit(solution)/shard_map/reduce_scatter | solution.py:293
  310.0 1.3 copy-start.4
  311.2 1.3 copy-start.5
  358.9 98.6 %all-to-all-start.3 = ((bf16[8,2,16,32,256]{4,3,2,1,0:T(8,128)(2,1)}), bf16[8,2,16,32,256]{4,3,2,1,0:T(8,128)(2,1)}, u32[]{:S(2)}, u32[]{:S(2)}) async-start(bf16[8,2,16,32,256]{4,3,2,1,0:T(8,128)(2,1)} %get-tuple-element.22), calls=%async_computation.5 | async-start | bytes 8388608 | tf_op jit(solution)/shard_map/all_to_all | solution.py:260
  428.2 1.4 copy-start.3
  431.5 1.1 copy-start
  457.5 42.5 %all-to-all-start.4 = ((bf16[32,8,8,384]{3,2,1,0:T(8,128)(2,1)}), bf16[32,8,8,384]{3,2,1,0:T(8,128)(2,1)}, u32[]{:S(2)}, u32[]{:S(2)}) async-start(bf16[32,8,8,384]{3,2,1,0:T(8,128)(2,1)} %bitcast.70), calls=%async_computation.6 | async-start | bytes 3145728 | tf_op jit(solution)/shard_map/all_to_all | solution.py:260
  502.6 1.1 copy-start.1
  503.7 23.8 %all-to-all-start.5 = ((bf16[4,8,64,384]{3,2,1,0:T(8,128)(2,1)}), bf16[4,8,64,384]{3,2,1,0:T(8,128)(2,1)}, u32[]{:S(2)}, u32[]{:S(2)}) async-start(bf16[4,8,64,384]{3,2,1,0:T(8,128)(2,1)} %copy-done.1), calls=%async_computation.7 | async-start | bytes 3145728 | tf_op jit(solution)/shard_map/all_to_all | solution.py:260
Sparse Core Ops, SparseCore 0:
  171.2 71.5 reduce-scatter.2
  359.0 69.0 reduce-scatter.4
